TPU v7x, 256 devices: a whole 4x4x8 slice. The times are simulated.
256 devices in a mesh: row: 16 (over z_lo, x), col: 16 (over z_hi, y, core).
Axes of the slice: x: 4, y: 4, z: 8 (z_hi: 2, z_lo: 4; z = z_hi * 4 + z_lo), core: 2. Of those that a mesh axis runs over, the one named last changes fastest.
Arguments:
- inverse_tiles: bfloat16 [16384, 16384], P('row', 'col'), may hold values from -0.046875 to 0.046875
- factor: bfloat16 [16384, 4, 512], P('row', None, 'col'), may hold values from -0.75 to 0.75
- inverse_diag: float32 [4, 512, 512], P(None, 'row', 'col'), may hold values from -6 to 6
- tile_list: int32 [4, 128], replicated, may hold values from 0 to 127, as said below
- tile_count: int32 [4], replicated, may hold values from 86 to 128, as said below
Outputs:
- inverse_panel: bfloat16 [16384, 4, 512], P(('row', 'col'))
- diag_block: float32 [4, 512, 512], P(None, 'row', 'col')
Inputs may be any that keep to these rules, and one draw needn't show every extreme that they name: For each supernode the first tile_count entries of tile_list name distinct tiles in increasing order; the remaining entries name the tiles that are not listed. `tile_count`: some supernode lists all 128 tiles.
All inputs are finite; a program needn't handle non-finite values.
Results may differ from a plain program's by a relative error of at most 0.014.
Values may be sent and summed in bfloat16 or wider, within the bound.
A program may use at most 64 MiB of HBM per device.

v0:
```python
import jax
import jax.numpy as jnp
from jax import lax
from jax.sharding import Mesh
from jax.sharding import PartitionSpec as P

TILE = 128
COL = ("col_0", "col_1", "col_2")
ROW_COL = ("row", "col_0", "col_1", "col_2")


def spread(x, axis, root):
    mine = lax.axis_index(axis) == root
    return lax.psum(jnp.where(mine, x, jnp.zeros_like(x)), axis)


def split_up(x, dim, size):
    before, after = (x.shape[:dim], x.shape[dim + 1 :])
    return jnp.moveaxis(x.reshape(*before, size, -1, *after), dim, 0)


def summed_rows(x, chips, core, dim):
    sizes = (lax.axis_size(chips), lax.axis_size(core))
    blocks = split_up(x, dim, sizes[0] * sizes[1])
    inside = blocks.shape[1:]
    blocks = blocks.reshape(*sizes, *inside).swapaxes(0, 1).reshape(-1, *inside)
    blocks = lax.psum_scatter(blocks, core, scatter_dimension=0, tiled=True)
    return lax.psum_scatter(blocks, chips, scatter_dimension=0, tiled=True)[0]


def sent_and_summed(x, axis, dim):
    blocks = split_up(x, dim, lax.axis_size(axis))
    arrived = lax.all_to_all(blocks, axis, split_axis=0, concat_axis=0, tiled=True)
    return arrived.astype(jnp.float32).sum(axis=0)


def per_device(inverse_tiles, factor, inverse_diag, tile_list, tile_count):
    row_devices = lax.axis_size("row")
    col_devices = lax.axis_size(COL)
    row_index = lax.axis_index("row")
    col_index = lax.axis_index(COL)
    rows_blk = inverse_tiles.shape[0]
    cols_blk = inverse_tiles.shape[1]
    supers = factor.shape[1]
    panel_width = factor.shape[2] * col_devices
    tile_total = tile_list.shape[1]
    position = jnp.arange(tile_total, dtype=jnp.int32)
    matches = (tile_list[:, :, None] == position[None, None, :]) & (
        position[None, :, None] < tile_count[:, None, None]
    )
    listed = jnp.any(matches, axis=1).astype(jnp.float32)
    live_all = jnp.repeat(listed, TILE, axis=1)
    row_live = lax.dynamic_slice_in_dim(live_all, row_index * rows_blk, rows_blk, 1).T
    row_factor = lax.all_gather(factor, COL, axis=2, tiled=True)
    row_factor = jnp.where(row_live[:, :, None] > 0, row_factor, jnp.zeros_like(row_factor))
    blocks_per = row_devices // col_devices
    received = spread(row_factor, "row", col_index * blocks_per + 0)
    col_factor = received.reshape(cols_blk, supers * panel_width)
    whole_term = jnp.dot(inverse_tiles, col_factor, preferred_element_type=jnp.float32).reshape(
        rows_blk, supers, panel_width
    )
    panel_cols = summed_rows(whole_term, ("col_0", "col_1"), "col_2", 2)
    panel_cols = -panel_cols * row_live[:, :, None]
    diag_part = jnp.einsum(
        "rsv,rsw->svw", row_factor.astype(jnp.float32), panel_cols, precision=lax.Precision.HIGHEST
    )
    diag_mine = sent_and_summed(diag_part.astype(jnp.bfloat16), "row", 1)
    inverse_panel = lax.all_to_all(
        panel_cols.astype(jnp.bfloat16), COL, split_axis=0, concat_axis=2, tiled=True
    )
    diag_block = inverse_diag - diag_mine
    return (inverse_panel, diag_block)


def solution(mesh):
    torus = Mesh(
        mesh.devices.reshape(mesh.shape["row"], 2, 4, 2), ("row", "col_0", "col_1", "col_2")
    )
    return jax.shard_map(
        per_device,
        mesh=torus,
        in_specs=(P("row", COL), P("row", None, COL), P(None, "row", COL), P(), P()),
        out_specs=(P(ROW_COL, None, None), P(None, "row", COL)),
        check_vma=False,
    )
```

profile of v0, /device:TPU:32, one launch (start us, length us, event | category | flops | bytes accessed | tf_op | source)
XLA Modules:
  0.0 482.2 jit_solution(6248333700501249892)
XLA Ops:
  7.2 0.0 copy-start
  7.2 0.0 all-gather.2.cloned.1.call-start
  7.2 0.7 all-gather.2.cloned.1.call-update
  7.9 0.0 all-reduce.2.cloned.1.call-start
  8.0 0.7 iota_compare_fusion.1
  8.7 0.9 fusion.6
  9.6 0.1 broadcast_bitcast_fusion
  9.7 0.2 copy.57
  9.9 79.6 %all-gather.2.cloned.1.call-done = bf16[1024,4,512]{0,2,1:T(8,128)(2,1)} async-done(((bf16[1024,4,32]{0,2,1:T(8,128)(2,1)}), bf16[1024,4,512]{0,2,1:T(8,128)(2,1)}) %all-gather.2.cloned.1.call-update) | async-done | bytes 4194320 | tf_op jit(solution)/shard_map/all_gather | solution.py:54
  89.5 4.5 broadcast_select_fusion.1
  94.1 0.0 all-reduce.2.cloned.1.call-update
  94.1 0.0 reduce-scatter.3.cloned.1.call-start
  94.1 169.6 %all-reduce.2.cloned.1.call-done = bf16[1024,2048]{0,1:T(8,128)(2,1)} async-done(((bf16[1024,2048]{0,1:T(8,128)(2,1)}), bf16[1024,2048]{0,1:T(8,128)(2,1)}) %all-reduce.2.cloned.1.call-update) | async-done | bytes 4194320 | tf_op jit(solution)/shard_map/psum | solution.py:14
  263.7 0.0 copy-done
  263.7 6.4 %fusion.9 = f32[2048,1024]{1,0:T(8,128)S(1)} fusion(bf16[1024,2048]{0,1:T(8,128)(2,1)} %all-reduce.2.cloned.1.call-done, bf16[1024,1024]{1,0:T(8,128)(2,1)S(1)} %copy-done), kind=kOutput, calls=%fused_computation.20 | convolution fusion | flops 4294967296 | bytes 14680064 | tf_op jit(solution)/shard_map/dot_general | solution.py:59
  270.1 4.1 copy.38
  274.2 0.0 reduce-scatter.3.cloned.1.call-update
  274.2 0.0 reduce-scatter.5.cloned.1.call-start
  274.3 25.8 %reduce-scatter.3.cloned.1.call-done = f32[8,1024,4,32]{1,3,2,0:T(8,128)} async-done(((f32[16,1024,4,32]{1,3,2,0:T(8,128)}), f32[8,1024,4,32]{1,3,2,0:T(8,128)}) %reduce-scatter.3.cloned.1.call-update) | async-done | bytes 4194320 | tf_op jit(solution)/shard_map/reduce_scatter | solution.py:27
  300.1 0.0 reduce-scatter.5.cloned.1.call-update
  300.1 131.2 %reduce-scatter.5.cloned.1.call-done = f32[1,1024,4,32]{1,3,2,0:T(8,128)} async-done(((f32[8,1024,4,32]{1,3,2,0:T(8,128)}), f32[1,1024,4,32]{1,3,2,0:T(8,128)}) %reduce-scatter.5.cloned.1.call-update) | async-done | bytes 524304 | tf_op jit(solution)/shard_map/reduce_scatter | solution.py:28
  431.3 6.0 %fusion.2 = bf16[4,512,32]{1,2,0:T(8,128)(2,1)S(1)} fusion(bf16[1024,4,512]{0,2,1:T(8,128)(2,1)} %all-gather.2.cloned.1.call-done, pred[1024,4]{0,1:T(4,128)(4,1)S(1)} %get-tuple-element.12, f32[1,1024,4,32]{1,3,2,0:T(8,128)} %reduce-scatter.5.cloned.1.call-done, f32[1024,4]{0,1:T(4,128)S(1)} %get-tuple-element.13), kind=kOutput, calls=%fused_computation.4 | convolution fusion | flops 807731200 | bytes 4870144 | tf_op jit(solution)/shard_map/rsv,rsw->svw/dot_general | solution.py:64
  437.3 0.3 reshape.53
  437.6 0.1 copy.58
  437.7 1.2 reshape.56
  438.9 5.8 %all-to-all-start.1 = ((bf16[16,2,2048]{2,1,0:T(2,128)(2,1)}), bf16[16,2,2048]{2,1,0:T(2,128)(2,1)S(1)}, u32[]{:S(2)}, u32[]{:S(2)}) async-start(bf16[16,2,2048]{2,1,0:T(2,128)(2,1)} %reshape.56), calls=%async_computation.3 | async-start | bytes 262144 | tf_op jit(solution)/shard_map/all_to_all | solution.py:33
  444.7 1.1 fusion.3
  445.8 0.7 copy.39
  446.5 1.7 reshape.54
  448.2 3.4 all-to-all-done.1
  451.6 5.4 %all-to-all-start = ((bf16[16,2,4096]{2,1,0:T(2,128)(2,1)}), bf16[16,2,4096]{2,1,0:T(2,128)(2,1)S(1)}, u32[]{:S(2)}, u32[]{:S(2)}) async-start(bf16[16,2,4096]{2,1,0:T(2,128)(2,1)} %reshape.54), calls=%async_computation.2 | async-start | bytes 524288 | tf_op jit(solution)/shard_map/all_to_all | solution.py:68
  457.0 0.9 copy.45
  457.9 0.3 reshape.57
  458.2 0.1 convert_reduce_fusion
  458.3 0.7 copy.47
  459.1 12.7 %all-to-all-done = bf16[16,2,4096]{2,1,0:T(2,128)(2,1)S(1)} async-done(((bf16[16,2,4096]{2,1,0:T(2,128)(2,1)}), bf16[16,2,4096]{2,1,0:T(2,128)(2,1)S(1)}, u32[]{:S(2)}, u32[]{:S(2)}) %all-to-all-start) | async-done | bytes 262176 | tf_op jit(solution)/shard_map/all_to_all | solution.py:68
  471.8 0.5 reshape.55
  472.3 1.3 copy.50
  473.6 2.0 copy.46
  (3 shorter events, 0.0 us)
Async XLA Ops:
  7.2 256.6 %copy-start = (bf16[1024,1024]{1,0:T(8,128)(2,1)S(1)}, bf16[1024,1024]{1,0:T(8,128)(2,1)}, u32[]{:S(2)}) copy-start(bf16[1024,1024]{1,0:T(8,128)(2,1)} %param.5) | copy-start | bytes 6291460
  7.2 82.4 %all-gather.2.cloned.1.call-start = ((), (), s32[]{:S(2)}) async-start(), calls=%async_computation.4 | async-start | bytes 4456448 | tf_op jit(solution)/shard_map/all_gather | solution.py:54
  7.9 255.8 %all-reduce.2.cloned.1.call-start = ((), (), s32[]{:S(2)}) async-start(), calls=%async_computation.5 | async-start | bytes 8388608 | tf_op jit(solution)/shard_map/psum | solution.py:14
  94.1 206.0 %reduce-scatter.3.cloned.1.call-start = ((), (), s32[]{:S(2)}) async-start(), calls=%async_computation.6 | async-start | bytes 12582912 | tf_op jit(solution)/shard_map/reduce_scatter | solution.py:27
  274.2 157.1 %reduce-scatter.5.cloned.1.call-start = ((), (), s32[]{:S(2)}) async-start(), calls=%async_computation.7 | async-start | bytes 4718592 | tf_op jit(solution)/shard_map/reduce_scatter | solution.py:28
  438.9 12.7 %all-to-all-start.1 = ((bf16[16,2,2048]{2,1,0:T(2,128)(2,1)}), bf16[16,2,2048]{2,1,0:T(2,128)(2,1)S(1)}, u32[]{:S(2)}, u32[]{:S(2)}) async-start(bf16[16,2,2048]{2,1,0:T(2,128)(2,1)} %reshape.56), calls=%async_computation.3 | async-start | bytes 262144 | tf_op jit(solution)/shard_map/all_to_all | solution.py:33
  451.6 20.2 %all-to-all-start = ((bf16[16,2,4096]{2,1,0:T(2,128)(2,1)}), bf16[16,2,4096]{2,1,0:T(2,128)(2,1)S(1)}, u32[]{:S(2)}, u32[]{:S(2)}) async-start(bf16[16,2,4096]{2,1,0:T(2,128)(2,1)} %reshape.54), calls=%async_computation.2 | async-start | bytes 524288 | tf_op jit(solution)/shard_map/all_to_all | solution.py:68
Sparse Core Ops, SparseCore 0:
  10.8 78.7 all-gather.1
  94.2 169.4 all-reduce.1
  274.3 25.6 reduce-scatter.2
  304.6 126.5 reduce-scatter.4
where the time goes:
time: 483 us; the launch traced here: 482 us
  waiting for transfers between devices  423 us (88%)
  local copies, waits for them, and re-layouts  14.1 us (3%)
  between operations  13.9 us (3%)
  matrix products  12.3 us (3%)
  starting transfers between devices  11.4 us (2%)
  other arithmetic  7.39 us (2%)
    psum x1, waiting for transfers between devices, spread(): return lax.psum(jnp.where(mine, x, jnp.zeros_like(x)), axis)  170 us
    reduce_scatter x1, waiting for transfers between devices, summed_rows(): return lax.psum_scatter(blocks, chips, scatter_dimension=0, tiled=True)[0]  131 us
    all_gather x1, waiting for transfers between devices, per_device(): row_factor = lax.all_gather(factor, COL, axis=2, tiled=True)  79.6 us
    reduce_scatter x1, waiting for transfers between devices, summed_rows(): blocks = lax.psum_scatter(blocks, core, scatter_dimension=0, tiled=True)  25.8 us
    all_to_all x1, waiting for transfers between devices, per_device(): lax.all_to_all(panel_cols.astype(jnp.bfloat16), COL, split_axis=0, concat...  12.7 us
  transfers between devices with their start and end apart: 6, of which 6 were waited for; matrix products, arithmetic and copies ran while one was open for 2% of the time, Pallas kernels for 0%

commit v1 on v0

--- a/solution.py
+++ b/solution.py
@@ -65,9 +65,11 @@
         "rsv,rsw->svw", row_factor.astype(jnp.float32), panel_cols, precision=lax.Precision.HIGHEST
     )
     diag_mine = sent_and_summed(diag_part.astype(jnp.bfloat16), "row", 1)
-    inverse_panel = lax.all_to_all(
-        panel_cols.astype(jnp.bfloat16), COL, split_axis=0, concat_axis=2, tiled=True
-    )
+    part = panel_cols.astype(jnp.bfloat16)
+    count = lax.axis_size(COL)
+    pieces = jnp.stack(jnp.split(part, count, axis=0), axis=0)
+    pieces = lax.all_to_all(pieces, COL, split_axis=0, concat_axis=0)
+    inverse_panel = jnp.concatenate(pieces, axis=2)
     diag_block = inverse_diag - diag_mine
     return (inverse_panel, diag_block)
 

time: 483 us -> 491 us (1.017)
  local copies, waits for them, and re-layouts: 14.1 us -> 21.1 us
    unnamed x11 -> x28, local copies, waits for them, and re-layouts: 7.55 us -> 15.8 us
  transfers between devices with their start and end apart: 6 -> 6, of which waited for: 6 -> 6; matrix products, arithmetic and copies ran while one was open for 2% -> 1% of each run, Pallas kernels for 0% -> 0%
where the time goes in v1:
time: 491 us; the launch traced here: 490 us
  waiting for transfers between devices  424 us (86%)
  local copies, waits for them, and re-layouts  21.1 us (4%)
  between operations  13.9 us (3%)
  matrix products  12.4 us (3%)
  starting transfers between devices  11.3 us (2%)
  other arithmetic  7.39 us (2%)
    psum x1, waiting for transfers between devices, spread(): return lax.psum(jnp.where(mine, x, jnp.zeros_like(x)), axis)  170 us
    reduce_scatter x1, waiting for transfers between devices, summed_rows(): return lax.psum_scatter(blocks, chips, scatter_dimension=0, tiled=True)[0]  131 us
    all_gather x1, waiting for transfers between devices, per_device(): row_factor = lax.all_gather(factor, COL, axis=2, tiled=True)  79.6 us
    reduce_scatter x1, waiting for transfers between devices, summed_rows(): blocks = lax.psum_scatter(blocks, core, scatter_dimension=0, tiled=True)  25.8 us
    unnamed x28, local copies, waits for them, and re-layouts  15.8 us
    all_to_all x1, waiting for transfers between devices, per_device(): pieces = lax.all_to_all(pieces, COL, split_axis=0, concat_axis=0)  13.6 us
  transfers between devices with their start and end apart: 6, of which 6 were waited for; matrix products, arithmetic and copies ran while one was open for 1% of the time, Pallas kernels for 0%

profile of v1, /device:TPU:32, one launch (start us, length us, event | category | flops | bytes accessed | tf_op | source)
XLA Modules:
  0.0 490.3 jit_solution(5882561430228716836)
XLA Ops:
  7.2 0.0 all-gather.2.cloned.1.call-start
  7.2 0.7 all-gather.2.cloned.1.call-update
  7.9 0.0 all-reduce.2.cloned.1.call-start
  8.0 0.7 iota_compare_fusion.1
  8.7 0.9 fusion.6
  9.6 0.1 broadcast_bitcast_fusion
  9.7 0.2 copy.51
  9.9 79.6 %all-gather.2.cloned.1.call-done = bf16[1024,4,512]{0,2,1:T(8,128)(2,1)} async-done(((bf16[1024,4,32]{0,2,1:T(8,128)(2,1)}), bf16[1024,4,512]{0,2,1:T(8,128)(2,1)}) %all-gather.2.cloned.1.call-update) | async-done | bytes 4194320 | tf_op jit(solution)/shard_map/all_gather | solution.py:54
  89.5 4.5 broadcast_select_fusion.1
  94.1 0.0 reduce-scatter.3.cloned.1.call-start
  94.1 169.6 %all-reduce.2.cloned.1.call-done = bf16[1024,2048]{0,1:T(8,128)(2,1)} async-done(((bf16[1024,2048]{0,1:T(8,128)(2,1)}), bf16[1024,2048]{0,1:T(8,128)(2,1)}) %all-reduce.2.cloned.1.call-update) | async-done | bytes 4194320 | tf_op jit(solution)/shard_map/psum | solution.py:14
  263.7 6.4 %fusion.9 = f32[2048,1024]{1,0:T(8,128)S(1)} fusion(bf16[1024,2048]{0,1:T(8,128)(2,1)} %all-reduce.2.cloned.1.call-done, bf16[1024,1024]{1,0:T(8,128)(2,1)S(1)} %copy-done), kind=kOutput, calls=%fused_computation.53 | convolution fusion | flops 4294967296 | bytes 14680064 | tf_op jit(solution)/shard_map/dot_general | solution.py:59
  270.1 4.1 copy.36
  274.2 0.0 reduce-scatter.5.cloned.1.call-start
  274.2 25.8 %reduce-scatter.3.cloned.1.call-done = f32[8,1024,4,32]{1,3,2,0:T(8,128)} async-done(((f32[16,1024,4,32]{1,3,2,0:T(8,128)}), f32[8,1024,4,32]{1,3,2,0:T(8,128)}) %reduce-scatter.3.cloned.1.call-update) | async-done | bytes 4194320 | tf_op jit(solution)/shard_map/reduce_scatter | solution.py:27
  300.1 131.5 %reduce-scatter.5.cloned.1.call-done = f32[1,1024,4,32]{1,3,2,0:T(8,128)} async-done(((f32[8,1024,4,32]{1,3,2,0:T(8,128)}), f32[1,1024,4,32]{1,3,2,0:T(8,128)}) %reduce-scatter.5.cloned.1.call-update) | async-done | bytes 524304 | tf_op jit(solution)/shard_map/reduce_scatter | solution.py:28
  431.5 1.1 fusion.3
  432.6 0.6 constant_dynamic-update-slice_fusion.15
  433.3 0.7 constant_dynamic-update-slice_fusion.14
  434.0 0.6 constant_dynamic-update-slice_fusion.13
  434.6 0.7 constant_dynamic-update-slice_fusion.12
  435.3 0.6 constant_dynamic-update-slice_fusion.11
  435.9 0.7 constant_dynamic-update-slice_fusion.10
  436.6 0.6 constant_dynamic-update-slice_fusion.9
  437.2 0.7 constant_dynamic-update-slice_fusion.8
  437.9 0.6 constant_dynamic-update-slice_fusion.7
  438.5 0.7 constant_dynamic-update-slice_fusion.6
  439.2 0.6 constant_dynamic-update-slice_fusion.5
  439.8 0.7 constant_dynamic-update-slice_fusion.4
  440.5 0.6 constant_dynamic-update-slice_fusion.3
  441.2 0.7 constant_dynamic-update-slice_fusion.2
  441.8 6.0 %fusion.2 = bf16[4,512,32]{1,2,0:T(8,128)(2,1)S(1)} fusion(bf16[1024,4,512]{0,2,1:T(8,128)(2,1)} %all-gather.2.cloned.1.call-done, pred[1024,4]{0,1:T(4,128)(4,1)S(1)} %get-tuple-element.8, f32[1,1024,4,32]{1,3,2,0:T(8,128)} %reduce-scatter.5.cloned.1.call-done, f32[1024,4]{0,1:T(4,128)S(1)} %get-tuple-element.9), kind=kOutput, calls=%fused_computation.4 | convolution fusion | flops 807731200 | bytes 4870144 | tf_op jit(solution)/shard_map/rsv,rsw->svw/dot_general | solution.py:64
  447.9 0.3 reshape.61
  448.2 0.1 copy.52
  448.3 1.2 reshape.64
  449.5 5.8 %all-to-all-start.1 = ((bf16[16,2,2048]{2,1,0:T(2,128)(2,1)}), bf16[16,2,2048]{2,1,0:T(2,128)(2,1)S(1)}, u32[]{:S(2)}, u32[]{:S(2)}) async-start(bf16[16,2,2048]{2,1,0:T(2,128)(2,1)} %reshape.64), calls=%async_computation.3 | async-start | bytes 262144 | tf_op jit(solution)/shard_map/all_to_all | solution.py:33
  455.3 0.6 constant_dynamic-update-slice_fusion.1
  455.9 0.7 constant_dynamic-update-slice_fusion
  456.6 2.1 reshape.62
  458.8 3.5 all-to-all-done.1
  462.2 5.4 %all-to-all-start = ((bf16[16,2,4096]{2,1,0:T(2,128)(2,1)}), bf16[16,2,4096]{2,1,0:T(2,128)(2,1)S(1)}, u32[]{:S(2)}, u32[]{:S(2)}) async-start(bf16[16,2,4096]{2,1,0:T(2,128)(2,1)} %reshape.62), calls=%async_computation.2 | async-start | bytes 524288 | tf_op jit(solution)/shard_map/all_to_all | solution.py:71
  467.6 0.1 copy.41
  467.7 0.3 reshape.65
  468.0 0.1 convert_reduce_fusion
  468.1 0.7 copy.43
  468.8 13.6 %all-to-all-done = bf16[16,2,4096]{2,1,0:T(2,128)(2,1)S(1)} async-done(((bf16[16,2,4096]{2,1,0:T(2,128)(2,1)}), bf16[16,2,4096]{2,1,0:T(2,128)(2,1)S(1)}, u32[]{:S(2)}, u32[]{:S(2)}) %all-to-all-start) | async-done | bytes 262176 | tf_op jit(solution)/shard_map/all_to_all | solution.py:71
  482.4 0.3 reshape.63
  482.8 1.0 copy.42
  (12 shorter events, 0.2 us)
Async XLA Ops:
  7.2 256.6 %copy-start = (bf16[1024,1024]{1,0:T(8,128)(2,1)S(1)}, bf16[1024,1024]{1,0:T(8,128)(2,1)}, u32[]{:S(2)}) copy-start(bf16[1024,1024]{1,0:T(8,128)(2,1)} %param.5) | copy-start | bytes 6291460
  7.2 82.4 %all-gather.2.cloned.1.call-start = ((), (), s32[]{:S(2)}) async-start(), calls=%async_computation.4 | async-start | bytes 4456448 | tf_op jit(solution)/shard_map/all_gather | solution.py:54
  7.9 255.8 %all-reduce.2.cloned.1.call-start = ((), (), s32[]{:S(2)}) async-start(), calls=%async_computation.5 | async-start | bytes 8388608 | tf_op jit(solution)/shard_map/psum | solution.py:14
  94.1 205.9 %reduce-scatter.3.cloned.1.call-start = ((), (), s32[]{:S(2)}) async-start(), calls=%async_computation.6 | async-start | bytes 12582912 | tf_op jit(solution)/shard_map/reduce_scatter | solution.py:27
  274.2 157.3 %reduce-scatter.5.cloned.1.call-start = ((), (), s32[]{:S(2)}) async-start(), calls=%async_computation.7 | async-start | bytes 4718592 | tf_op jit(solution)/shard_map/reduce_scatter | solution.py:28
  441.8 25.8 %copy-start.1 = (f32[4,32,32]{2,1,0:T(8,128)S(1)}, f32[4,32,32]{2,1,0:T(8,128)}, u32[]{:S(2)}) copy-start(f32[4,32,32]{2,1,0:T(8,128)} %param.7) | copy-start | bytes 49156
  449.5 12.7 %all-to-all-start.1 = ((bf16[16,2,2048]{2,1,0:T(2,128)(2,1)}), bf16[16,2,2048]{2,1,0:T(2,128)(2,1)S(1)}, u32[]{:S(2)}, u32[]{:S(2)}) async-start(bf16[16,2,2048]{2,1,0:T(2,128)(2,1)} %reshape.64), calls=%async_computation.3 | async-start | bytes 262144 | tf_op jit(solution)/shard_map/all_to_all | solution.py:33
  462.2 20.2 %all-to-all-start = ((bf16[16,2,4096]{2,1,0:T(2,128)(2,1)}), bf16[16,2,4096]{2,1,0:T(2,128)(2,1)S(1)}, u32[]{:S(2)}, u32[]{:S(2)}) async-start(bf16[16,2,4096]{2,1,0:T(2,128)(2,1)} %reshape.62), calls=%async_computation.2 | async-start | bytes 524288 | tf_op jit(solution)/shard_map/all_to_all | solution.py:71
Sparse Core Ops, SparseCore 0:
  10.8 78.7 all-gather.1
  94.2 169.4 all-reduce.1
  274.3 25.6 reduce-scatter.2
  304.6 126.8 reduce-scatter.4
